TPU v7x, 512 devices: a whole 4x8x8 slice. The times are simulated.
512 devices in a mesh: dom: 64 (over y, x, core), feat: 8 (over z).
Axes of the slice: x: 4, y: 8, z: 8, core: 2. Of those that a mesh axis runs over, the one named last changes fastest.
Arguments:
- features: bfloat16 [512, 196608], P('feat', 'dom'), may hold values from -16 to 16
- weights: bfloat16 [2, 512, 512], replicated, may hold values from -0.1875 to 0.1875
- tile_values: bfloat16 [4608, 128, 128], P('dom'), may hold values from 0 to 0.099609375
- tile_blocks: int32 [4608, 2], P('dom'), may hold values from 0 to 31
- tile_counts: int32 [64], P('dom'), may hold values from 36 to 72
- replica: int32 [64, 64, 16], P('dom'), may hold values from -1 to 3071, as said below
- cotangent: bfloat16 [512, 196608], P(None, ('dom', 'feat')), may hold values from -6 to 6
Outputs:
- output: bfloat16 [512, 196608], P(None, ('dom', 'feat'))
- feature_grad: bfloat16 [512, 196608], P('feat', 'dom')
- weight_grad: float32 [2, 512, 512], P(None, 'feat')
Inputs may be any that keep to these rules, and one draw needn't show every extreme that they name: `tile_blocks`: column 0 names a tile's source block and column 1 its destination block. replica[q, p, k] is the master slot on partition q of the vertex in mirror slot q * 16 + k of partition p, or -1 for an unused slot; the used slots of a pair (q, p) come first; no partition mirrors its own masters; each master partition fills all 16 slots toward at least one partition.
All inputs are finite; a program needn't handle non-finite values.
Results may differ from a plain program's by a relative error of at most 0.0058.
Values may be sent and summed in bfloat16 or wider, within the bound.
A program may use at most 64 MiB of HBM per device.

v0:
```python
import jax
import jax.numpy as jnp
from jax import lax
from jax.sharding import PartitionSpec as P


def gathered_total(x, axis):
    pieces = lax.all_gather(x, axis).astype(jnp.float32)
    return pieces.sum(axis=0)


def local(features, weights, tile_values, tile_blocks, tile_counts, replica, cotangent):
    feat_width, masters = features.shape
    tile_size = tile_values.shape[1]
    replica_rows = replica[0]
    slot_used = (replica_rows >= 0).reshape(-1)
    slot_index = jnp.where(replica_rows >= 0, replica_rows, 0).reshape(-1)
    tile_live = (jnp.arange(tile_values.shape[0]) < tile_counts[0]).astype(jnp.float32)
    source_blocks = tile_blocks[:, 0]
    target_blocks = tile_blocks[:, 1]

    def pull_mirrors(values_in):
        outgoing = jnp.where(
            slot_used[None, :],
            jnp.take(values_in, slot_index, axis=1),
            jnp.zeros((), values_in.dtype),
        )
        return lax.all_to_all(outgoing, "dom", split_axis=1, concat_axis=1, tiled=True)

    def push_mirrors(partial_value):
        incoming = lax.all_to_all(
            partial_value[:, masters:].astype(jnp.bfloat16),
            "dom",
            split_axis=1,
            concat_axis=1,
            tiled=True,
        ).astype(jnp.float32)
        targets = jnp.where(slot_used, slot_index, masters)
        return partial_value[:, :masters].at[:, targets].add(incoming, mode="drop")

    def spread(own_cols, forward):
        local_cols = jnp.concatenate([own_cols, pull_mirrors(own_cols)], 1)
        nblocks = local_cols.shape[1] // tile_size
        blocks = local_cols.reshape(feat_width, nblocks, tile_size)
        if forward:
            picked = jnp.take(blocks, source_blocks, axis=1)
            contrib = jnp.einsum(
                "fts,tsd->ftd", picked, tile_values, preferred_element_type=jnp.float32
            )
            segment = target_blocks
        else:
            picked = jnp.take(blocks, target_blocks, axis=1)
            contrib = jnp.einsum(
                "ftd,tsd->fts", picked, tile_values, preferred_element_type=jnp.float32
            )
            segment = source_blocks
        onehot = (segment[:, None] == jnp.arange(nblocks)[None, :]).astype(jnp.float32) * tile_live[
            :, None
        ]
        partial_value = jnp.einsum("ftd,tb->fbd", contrib, onehot, precision=lax.Precision.HIGHEST)
        return push_mirrors(partial_value.reshape(feat_width, nblocks * tile_size))

    aggregate = spread(features, True).astype(jnp.bfloat16)
    feat_rows, agg_rows = (
        lax.all_to_all(features, "feat", split_axis=1, concat_axis=0, tiled=True),
        lax.all_to_all(aggregate, "feat", split_axis=1, concat_axis=0, tiled=True),
    )
    preact = jnp.einsum("io,iv->ov", weights[0], feat_rows, preferred_element_type=jnp.float32)
    preact = preact + jnp.einsum(
        "io,iv->ov", weights[1], agg_rows, preferred_element_type=jnp.float32
    )
    sigmoid_z = jax.nn.sigmoid(preact)
    output = (preact * sigmoid_z).astype(jnp.bfloat16)
    slope = sigmoid_z * (1.0 + preact * (1.0 - sigmoid_z))
    pre_grad = (cotangent.astype(jnp.float32) * slope).astype(jnp.bfloat16)
    slice_start = lax.axis_index("feat") * feat_width
    grad_cols = lax.all_gather(pre_grad, "feat", axis=1, tiled=True)
    weight_slice = lax.dynamic_slice_in_dim(weights, slice_start, feat_width, 1)
    terms = jnp.stack(
        [
            jnp.einsum("iv,ov->io", features, grad_cols, preferred_element_type=jnp.float32),
            jnp.einsum("iv,ov->io", aggregate, grad_cols, preferred_element_type=jnp.float32),
        ]
    )
    weight_grad = gathered_total(terms.astype(jnp.bfloat16), "dom").astype(jnp.float32)
    back_slices = jnp.einsum(
        "kio,ov->kiv", weight_slice, grad_cols, preferred_element_type=jnp.float32
    ).astype(jnp.bfloat16)
    self_grad = back_slices[0]
    agg_grad = back_slices[1]
    back_terms = spread(agg_grad, False)
    feature_grad = (self_grad.astype(jnp.float32) + back_terms).astype(jnp.bfloat16)
    return (output, feature_grad, weight_grad)


def solution(mesh):
    return jax.shard_map(
        local,
        mesh=mesh,
        in_specs=(
            P("feat", "dom"),
            P(),
            P("dom", None, None),
            P("dom", None),
            P("dom"),
            P("dom", None, None),
            P(None, ("dom", "feat")),
        ),
        out_specs=(P(None, ("dom", "feat")), P("feat", "dom"), P(None, "feat", None)),
        check_vma=False,
    )
```

profile of v0, /device:TPU:1, one launch (start us, length us, event | category | flops | bytes accessed | tf_op | source)
XLA Modules:
  0.0 258.0 jit_solution(7112404868492813658)
XLA Ops:
  10.1 4.3 %gather_fusion = bf16[1024,64]{1,0:T(8,128)(2,1)} fusion(bf16[64,3072]{0,1:T(8,128)(2,1)S(1)} %copy.72, s32[1024]{0:T(1024)S(1)} %fusion.34), kind=kCustom, calls=%fused_computation.clone | custom fusion | bytes 266240 | tf_op jit(solution)/shard_map/jit(_take)/gather | solution.py:25
  16.6 11.6 %all-to-all-start.1 = ((bf16[64,2,512]{2,1,0:T(2,128)(2,1)}), bf16[64,2,512]{2,1,0:T(2,128)(2,1)S(1)}, u32[]{:S(2)}, u32[]{:S(2)}) async-start(bf16[64,2,512]{2,1,0:T(2,128)(2,1)} %reshape.201), calls=%async_computation.1 | async-start | bytes 262144 | tf_op jit(solution)/shard_map/all_to_all | solution.py:28
  30.8 8.6 %all-to-all-done.1 = bf16[64,2,512]{2,1,0:T(2,128)(2,1)S(1)} async-done(((bf16[64,2,512]{2,1,0:T(2,128)(2,1)}), bf16[64,2,512]{2,1,0:T(2,128)(2,1)S(1)}, u32[]{:S(2)}, u32[]{:S(2)}) %all-to-all-start.1) | async-done | bytes 131104 | tf_op jit(solution)/shard_map/all_to_all | solution.py:28
  39.9 1.8 gather_fusion.1
  41.7 2.1 convolution_bitcast_fusion.1
  43.8 2.7 %fusion.3 = f32[32,64,128]{2,0,1:T(8,128)S(1)} fusion(f32[64,72,128]{2,0,1:T(8,128)S(1)} %convolution_bitcast_fusion.1, f32[72]{0:T(128)S(1)} %compare_convert_fusion, s32[72]{0:T(128)S(1)} %get-tuple-element.29), kind=kOutput, calls=%fused_computation.11 | convolution fusion | flops 226497024 | bytes 3408448 | tf_op jit(solution)/shard_map/ftd,tb->fbd/dot_general | solution.py:60
  49.1 4.4 %all-to-all-start.2 = ((bf16[64,2,512]{2,1,0:T(2,128)(2,1)}), bf16[64,2,512]{2,1,0:T(2,128)(2,1)S(1)}, u32[]{:S(2)}, u32[]{:S(2)}) async-start(bf16[64,2,512]{2,1,0:T(2,128)(2,1)} %reshape.203), calls=%async_computation.2 | async-start | bytes 262144 | tf_op jit(solution)/shard_map/all_to_all | solution.py:31
  54.3 10.6 %all-to-all-done.2 = bf16[64,2,512]{2,1,0:T(2,128)(2,1)S(1)} async-done(((bf16[64,2,512]{2,1,0:T(2,128)(2,1)}), bf16[64,2,512]{2,1,0:T(2,128)(2,1)S(1)}, u32[]{:S(2)}, u32[]{:S(2)}) %all-to-all-start.2) | async-done | bytes 131104 | tf_op jit(solution)/shard_map/all_to_all | solution.py:31
  64.9 10.0 %all-to-all-start = ((bf16[64,8,384]{2,0,1:T(8,128)(2,1)}), bf16[64,8,384]{2,0,1:T(8,128)(2,1)}, u32[]{:S(2)}, u32[]{:S(2)}) async-start(bf16[64,8,384]{2,0,1:T(8,128)(2,1)} %bitcast.122), calls=%async_computation | async-start | bytes 786432 | tf_op jit(solution)/shard_map/all_to_all | solution.py:65
  76.8 1.6 copy.78
  79.6 8.2 %scatter_custom_fusion = f32[64,3072]{0,1:T(8,128)} fusion(f32[64,3072]{0,1:T(8,128)} %copy.78, s32[1024]{0:T(1024)} %bitcast.140, bf16[64,1024]{0,1:T(8,128)(2,1)S(1)} %bitcast.133), kind=kCustom, calls=%fused_computation.42 | custom fusion | flops 131072 | bytes 917504 | tf_op jit(solution)/shard_map/scatter-add | solution.py:39
  87.8 1.5 convert_element_type.61
  90.3 6.6 %all-to-all-start.3 = ((bf16[64,8,384]{2,0,1:T(8,128)(2,1)}), bf16[64,8,384]{2,0,1:T(8,128)(2,1)}, u32[]{:S(2)}, u32[]{:S(2)}) async-start(bf16[64,8,384]{2,0,1:T(8,128)(2,1)} %copy.79), calls=%async_computation.3 | async-start | bytes 786432 | tf_op jit(solution)/shard_map/all_to_all | solution.py:66
  97.2 2.5 fusion.19
  99.7 10.8 %all-to-all-done.3 = bf16[64,8,384]{2,0,1:T(8,128)(2,1)} async-done(((bf16[64,8,384]{2,0,1:T(8,128)(2,1)}), bf16[64,8,384]{2,0,1:T(8,128)(2,1)}, u32[]{:S(2)}, u32[]{:S(2)}) %all-to-all-start.3) | async-done | bytes 393248 | tf_op jit(solution)/shard_map/all_to_all | solution.py:66
  110.4 3.1 %multiply_convert_fusion = (bf16[512,384]{1,0:T(8,128)(2,1)}, bf16[512,384]{1,0:T(8,128)(2,1)}) fusion(bf16[512,384]{1,0:T(8,128)(2,1)} %param.17, f32[512,384]{1,0:T(8,128)} %fusion.19, bf16[512,384]{1,0:T(8,128)(2,1)} %bitcast.19, bf16[2,512,512]{2,1,0:T(8,128)(2,1)} %param.12), kind=kOutput, calls=%fused_computation.30 | convolution fusion | flops 203882496 | bytes 2883584 | tf_op jit(solution)/shard_map/io,iv->ov/dot_general | solution.py:69
  113.6 38.6 %all-gather.3.cloned.1.call-done = bf16[512,3072]{1,0:T(8,128)(2,1)} async-done(((bf16[512,384]{1,0:T(8,128)(2,1)}), bf16[512,3072]{1,0:T(8,128)(2,1)}) %all-gather.3.cloned.1.call-update) | async-done | bytes 3145744 | tf_op jit(solution)/shard_map/all_gather | solution.py:77
  152.2 3.1 %fusion.13 = bf16[1,1,64,512]{3,2,1,0:T(8,128)(2,1)S(1)} fusion(bf16[64,3072]{0,1:T(8,128)(2,1)S(1)} %convert_element_type.61, bf16[512,3072]{1,0:T(8,128)(2,1)} %all-gather.3.cloned.1.call-done), kind=kOutput, calls=%fused_computation.26 | convolution fusion | flops 201359360 | bytes 3604480 | tf_op jit(solution)/shard_map/iv,ov->io/dot_general | solution.py:82
  157.1 2.6 convolution_convert_fusion
  161.0 4.3 %gather_fusion.2 = bf16[1024,64]{1,0:T(8,128)(2,1)} fusion(bf16[64,3072]{0,1:T(8,128)(2,1)S(1)} %copy.81, s32[1024]{0:T(1024)S(1)} %fusion.34), kind=kCustom, calls=%fused_computation.2.clone | custom fusion | bytes 266240 | tf_op jit(solution)/shard_map/jit(_take)/gather | solution.py:25
  166.8 22.9 %all_to_all.80 = bf16[64,2,512]{2,1,0:T(2,128)(2,1)S(1)} all-to-all(bf16[64,2,512]{2,1,0:T(2,128)(2,1)S(1)} %reshape.205), channel_id=1, replica_groups=mesh['dom'=64,'feat'=8] {'dom'}, dimensions={0} | all-to-all | bytes 262144 | tf_op jit(solution)/shard_map/all_to_all | solution.py:28
  190.2 1.9 gather_fusion.3
  192.1 3.0 %convolution_bitcast_fusion = f32[64,72,128]{2,0,1:T(8,128)S(1)} fusion(bf16[72,128,128]{2,1,0:T(8,128)(2,1)S(1)} %copy-done, bf16[72,64,128]{2,1,0:T(8,128)(2,1)} %gather_fusion.3, pred[72]{0:T(512)(128)(4,1)S(1)} %copy-done.11), kind=kOutput, calls=%fused_computation.13 | convolution fusion | flops 151584768 | bytes 5898312 | tf_op jit(solution)/shard_map/ftd,tsd->fts/dot_general | solution.py:53
  195.1 2.7 %fusion.1 = f32[32,64,128]{2,0,1:T(8,128)S(1)} fusion(f32[64,72,128]{2,0,1:T(8,128)S(1)} %convolution_bitcast_fusion, s32[72]{0:T(128)S(1)} %copy-done.12, f32[72]{0:T(128)S(1)} %copy-done.10), kind=kOutput, calls=%fused_computation.9 | convolution fusion | flops 226497024 | bytes 3408448 | tf_op jit(solution)/shard_map/ftd,tb->fbd/dot_general | solution.py:60
  199.3 1.8 reshape.207
  201.0 4.5 %all-to-all-start.5 = ((bf16[64,2,512]{2,1,0:T(2,128)(2,1)}), bf16[64,2,512]{2,1,0:T(2,128)(2,1)S(1)}, u32[]{:S(2)}, u32[]{:S(2)}) async-start(bf16[64,2,512]{2,1,0:T(2,128)(2,1)} %reshape.207), calls=%async_computation.5 | async-start | bytes 262144 | tf_op jit(solution)/shard_map/all_to_all | solution.py:31
  205.5 1.9 slice_add_fusion
  207.5 2.8 %copy.86 = f32[64,3072]{0,1:T(8,128)} copy(f32[64,3072]{1,0:T(8,128)} %slice_add_fusion) | data formatting | bytes 1572864 | tf_op jit(solution)/shard_map/add
  210.3 6.6 %all-to-all-done.5 = bf16[64,2,512]{2,1,0:T(2,128)(2,1)S(1)} async-done(((bf16[64,2,512]{2,1,0:T(2,128)(2,1)}), bf16[64,2,512]{2,1,0:T(2,128)(2,1)S(1)}, u32[]{:S(2)}, u32[]{:S(2)}) %all-to-all-start.5) | async-done | bytes 131104 | tf_op jit(solution)/shard_map/all_to_all | solution.py:31
  217.1 8.2 %scatter_custom_fusion.1 = f32[64,3072]{0,1:T(8,128)} fusion(f32[64,3072]{0,1:T(8,128)} %copy.86, s32[1024]{0:T(1024)} %bitcast.141, bf16[64,1024]{0,1:T(8,128)(2,1)S(1)} %bitcast.132), kind=kCustom, calls=%fused_computation.40 | custom fusion | flops 131072 | bytes 917504 | tf_op jit(solution)/shard_map/scatter-add | solution.py:39
  227.8 17.9 %all-gather.5.cloned.1.call-done = bf16[64,2,64,512]{3,2,1,0:T(8,128)(2,1)} async-done(((bf16[1,2,64,512]{3,2,1,0:T(8,128)(2,1)}), bf16[64,2,64,512]{3,2,1,0:T(8,128)(2,1)}) %all-gather.5.cloned.1.call-update) | async-done | bytes 8388624 | tf_op jit(solution)/shard_map/all_gather | solution.py:8
  245.7 5.5 %convert_reduce_fusion = f32[2,64,512]{2,1,0:T(8,128)} fusion(bf16[64,2,64,512]{3,2,1,0:T(8,128)(2,1)} %all-gather.5.cloned.1.call-done), kind=kLoop, calls=%fused_computation.6 | loop fusion | flops 8323072 | bytes 8650752 | tf_op jit(solution)/shard_map/reduce_sum | solution.py:9
  (70 shorter events, 24.3 us)
Async XLA Ops:
  7.2 34.5 %copy-start = (bf16[72,128,128]{2,1,0:T(8,128)(2,1)S(1)}, bf16[72,128,128]{2,1,0:T(8,128)(2,1)}, u32[]{:S(2)}) copy-start(bf16[72,128,128]{2,1,0:T(8,128)(2,1)} %param.13) | copy-start | bytes 7077892
  7.2 32.5 %copy-start.2 = (bf16[64,3072]{1,0:T(8,128)(2,1)S(1)}, bf16[64,3072]{1,0:T(8,128)(2,1)}, u32[]{:S(2)}) copy-start(bf16[64,3072]{1,0:T(8,128)(2,1)} %param.11) | copy-start | bytes 1179652
  7.2 21.0 %copy-start.8 = (s32[72,2]{0,1:T(2,128)S(1)}, s32[72,2]{0,1:T(2,128)}, u32[]{:S(2)}) copy-start(s32[72,2]{0,1:T(2,128)} %param.14) | copy-start | bytes 1732
  8.1 0.6 copy-start.6
  16.6 22.7 %all-to-all-start.1 = ((bf16[64,2,512]{2,1,0:T(2,128)(2,1)}), bf16[64,2,512]{2,1,0:T(2,128)(2,1)S(1)}, u32[]{:S(2)}, u32[]{:S(2)}) async-start(bf16[64,2,512]{2,1,0:T(2,128)(2,1)} %reshape.201), calls=%async_computation.1 | async-start | bytes 262144 | tf_op jit(solution)/shard_map/all_to_all | solution.py:28
  29.5 14.3 %copy-start.9 = (f32[72]{0:T(128)}, f32[72]{0:T(128)S(1)}, u32[]{:S(2)}) copy-start(f32[72]{0:T(128)S(1)} %compare_convert_fusion) | copy-start | bytes 868
  46.4 28.5 %copy-start.7 = (s32[1,64,16]{2,1,0:T(8,128)S(1)}, s32[1,64,16]{2,1,0:T(8,128)}, u32[]{:S(2)}) copy-start(s32[1,64,16]{2,1,0:T(8,128)} %copy-done.6) | copy-start | bytes 12292
  47.1 1.0 copy-start.3
  49.1 15.8 %all-to-all-start.2 = ((bf16[64,2,512]{2,1,0:T(2,128)(2,1)}), bf16[64,2,512]{2,1,0:T(2,128)(2,1)S(1)}, u32[]{:S(2)}, u32[]{:S(2)}) async-start(bf16[64,2,512]{2,1,0:T(2,128)(2,1)} %reshape.203), calls=%async_computation.2 | async-start | bytes 262144 | tf_op jit(solution)/shard_map/all_to_all | solution.py:31
  64.9 10.1 %copy-start.5 = (bf16[64,2,512]{2,1,0:T(2,128)(2,1)}, bf16[64,2,512]{2,1,0:T(2,128)(2,1)S(1)}, u32[]{:S(2)}) copy-start(bf16[64,2,512]{2,1,0:T(2,128)(2,1)S(1)} %all-to-all-done.2) | copy-start | bytes 393220
  64.9 25.4 %all-to-all-start = ((bf16[64,8,384]{2,0,1:T(8,128)(2,1)}), bf16[64,8,384]{2,0,1:T(8,128)(2,1)}, u32[]{:S(2)}, u32[]{:S(2)}) async-start(bf16[64,8,384]{2,0,1:T(8,128)(2,1)} %bitcast.122), calls=%async_computation | async-start | bytes 786432 | tf_op jit(solution)/shard_map/all_to_all | solution.py:65
  90.3 20.1 %all-to-all-start.3 = ((bf16[64,8,384]{2,0,1:T(8,128)(2,1)}), bf16[64,8,384]{2,0,1:T(8,128)(2,1)}, u32[]{:S(2)}, u32[]{:S(2)}) async-start(bf16[64,8,384]{2,0,1:T(8,128)(2,1)} %copy.79), calls=%async_computation.3 | async-start | bytes 786432 | tf_op jit(solution)/shard_map/all_to_all | solution.py:66
  96.9 55.3 %all-gather.3.cloned.1.call-start = ((), (), s32[]{:S(2)}) async-start(), calls=%async_computation.6 | async-start | bytes 3538944 | tf_op jit(solution)/shard_map/all_gather | solution.py:77
  113.6 132.1 %all-gather.5.cloned.1.call-start = ((), (), s32[]{:S(2)}) async-start(), calls=%async_computation.7 | async-start | bytes 8519680 | tf_op jit(solution)/shard_map/all_gather | solution.py:8
  152.2 3.1 %copy-start.1 = (bf16[512,3072]{1,0:T(8,128)(2,1)S(1)}, bf16[512,3072]{1,0:T(8,128)(2,1)}, u32[]{:S(2)}) copy-start(bf16[512,3072]{1,0:T(8,128)(2,1)} %all-gather.3.cloned.1.call-done) | copy-start | bytes 9437188
  159.6 0.9 copy-start.4
  166.6 25.5 %copy-start.11 = (pred[72]{0:T(512)(128)(4,1)S(1)}, pred[72]{0:T(512)(128)(4,1)}, u32[]{:S(2)}) copy-start(pred[72]{0:T(512)(128)(4,1)} %get-tuple-element.20) | copy-start | bytes 220
  192.1 3.0 %copy-start.10 = (f32[72]{0:T(128)S(1)}, f32[72]{0:T(128)}, u32[]{:S(2)}) copy-start(f32[72]{0:T(128)} %copy-done.9) | copy-start | bytes 868
  192.1 3.0 %copy-start.12 = (s32[72]{0:T(128)S(1)}, s32[72]{0:T(128)}, u32[]{:S(2)}) copy-start(s32[72]{0:T(128)} %get-tuple-element.28) | copy-start | bytes 868
  201.0 15.8 %all-to-all-start.5 = ((bf16[64,2,512]{2,1,0:T(2,128)(2,1)}), bf16[64,2,512]{2,1,0:T(2,128)(2,1)S(1)}, u32[]{:S(2)}, u32[]{:S(2)}) async-start(bf16[64,2,512]{2,1,0:T(2,128)(2,1)} %reshape.207), calls=%async_computation.5 | async-start | bytes 262144 | tf_op jit(solution)/shard_map/all_to_all | solution.py:31
Sparse Core Ops, SparseCore 0:
  113.7 38.4 all-gather.2
  157.2 88.4 all-gather.4
where the time goes:
time: 259 us; the launch traced here: 258 us
  waiting for transfers between devices  92.9 us (36%)
  starting transfers between devices  37.5 us (14%)
  local copies, waits for them, and re-layouts  35.4 us (14%)
  other arithmetic  31.5 us (12%)
  blocking collectives  22.9 us (9%)
  matrix products  22.7 us (9%)
  between operations  15 us (6%)
    all_gather x1, waiting for transfers between devices, local(): grad_cols = lax.all_gather(pre_grad, 'feat', axis=1, tiled=True)  38.6 us
    all_to_all x1, blocking collectives, pull_mirrors(): lax.all_to_all(outgoing, 'dom', split_axis=1, concat_axis=1, tiled=True)  22.9 us
    all_gather x1, waiting for transfers between devices, gathered_total(): pieces = lax.all_gather(x, axis).astype(jnp.float32)  17.9 us
    all_to_all x2, waiting for transfers between devices, push_mirrors(): lax.all_to_all(partial_value[:, masters:].astype(jnp.bfloat16), 'dom', sp...  17.1 us
    scatter-add x2, other arithmetic, push_mirrors(): return partial_value[:, :masters].at[:, targets].add(incoming, mode='drop')  16.4 us
    unnamed x39, local copies, waits for them, and re-layouts  12.5 us
    all_to_all x1, starting transfers between devices, pull_mirrors(): lax.all_to_all(outgoing, 'dom', split_axis=1, concat_axis=1, tiled=True)  11.6 us
    all_to_all x1, waiting for transfers between devices, local(): lax.all_to_all(aggregate, 'feat', split_axis=1, concat_axis=0, tiled=True)  10.8 us
  transfers between devices with their start and end apart: 7, of which 6 were waited for; matrix products, arithmetic and copies ran while one was open for 22% of the time, Pallas kernels for 0%

commit v1 on v0

--- a/solution.py
+++ b/solution.py
@@ -62,7 +62,12 @@
 
     aggregate = spread(features, True).astype(jnp.bfloat16)
     feat_rows, agg_rows = (
-        lax.all_to_all(features, "feat", split_axis=1, concat_axis=0, tiled=True),
+        jnp.concatenate(
+            lax.all_to_all(
+                jnp.stack(jnp.split(features, lax.axis_size("feat"), axis=1)), "feat", 0, 0
+            ),
+            axis=0,
+        ),
         lax.all_to_all(aggregate, "feat", split_axis=1, concat_axis=0, tiled=True),
     )
     preact = jnp.einsum("io,iv->ov", weights[0], feat_rows, preferred_element_type=jnp.float32)

time: 259 us -> 258 us (level)
  blocking collectives: 22.9 us -> 0 us
  starting transfers between devices: 37.5 us -> 48.1 us
  local copies, waits for them, and re-layouts: 35.4 us -> 43.4 us
  waiting for transfers between devices: 92.9 us -> 96.1 us
    all_to_all x1 -> x0, blocking collectives: 22.9 us -> none  [pull_mirrors(): lax.all_to_all(outgoing, 'dom', split_axis=1, concat_axis=1, tiled=True)]
    all_to_all x1 -> x2, starting transfers between devices: 11.6 us -> 22 us  [pull_mirrors(): lax.all_to_all(outgoing, 'dom', split_axis=1, concat_axis=1, tiled=True)]
    unnamed x39 -> x48, local copies, waits for them, and re-layouts: 12.5 us -> 21.4 us
    all_to_all x1 -> x2, waiting for transfers between devices: 8.57 us -> 15.4 us  [pull_mirrors(): lax.all_to_all(outgoing, 'dom', split_axis=1, concat_axis=1, tiled=True)]
  transfers between devices with their start and end apart: 7 -> 8, of which waited for: 6 -> 7; matrix products, arithmetic and copies ran while one was open for 22% -> 25% of each run, Pallas kernels for 0% -> 0%
where the time goes in v1:
time: 258 us; the launch traced here: 257 us
  waiting for transfers between devices  96.1 us (37%)
  starting transfers between devices  48.1 us (19%)
  local copies, waits for them, and re-layouts  43.4 us (17%)
  other arithmetic  31.6 us (12%)
  matrix products  22.4 us (9%)
  between operations  15 us (6%)
    all_gather x1, waiting for transfers between devices, local(): grad_cols = lax.all_gather(pre_grad, 'feat', axis=1, tiled=True)  39.7 us
    all_to_all x2, starting transfers between devices, pull_mirrors(): lax.all_to_all(outgoing, 'dom', split_axis=1, concat_axis=1, tiled=True)  22 us
    unnamed x48, local copies, waits for them, and re-layouts  21.4 us
    all_to_all x2, waiting for transfers between devices, push_mirrors(): lax.all_to_all(partial_value[:, masters:].astype(jnp.bfloat16), 'dom', sp...  16.4 us
    scatter-add x2, other arithmetic, push_mirrors(): return partial_value[:, :masters].at[:, targets].add(incoming, mode='drop')  16.4 us
    all_gather x1, waiting for transfers between devices, gathered_total(): pieces = lax.all_gather(x, axis).astype(jnp.float32)  15.6 us
    all_to_all x2, waiting for transfers between devices, pull_mirrors(): lax.all_to_all(outgoing, 'dom', split_axis=1, concat_axis=1, tiled=True)  15.4 us
    all_to_all x1, starting transfers between devices, local(): lax.all_to_all(jnp.stack(jnp.split(features, lax.axis_size('feat'), axis=...  10 us
  transfers between devices with their start and end apart: 8, of which 7 were waited for; matrix products, arithmetic and copies ran while one was open for 25% of the time, Pallas kernels for 0%

profile of v1, /device:TPU:1, one launch (start us, length us, event | category | flops | bytes accessed | tf_op | source)
XLA Modules:
  0.0 256.7 jit_solution(17932890263822669511)
XLA Ops:
  10.1 4.3 %gather_fusion = bf16[1024,64]{1,0:T(8,128)(2,1)} fusion(bf16[64,3072]{0,1:T(8,128)(2,1)S(1)} %copy.77, s32[1024]{0:T(1024)S(1)} %fusion.34), kind=kCustom, calls=%fused_computation.clone | custom fusion | bytes 266240 | tf_op jit(solution)/shard_map/jit(_take)/gather | solution.py:25
  16.6 11.6 %all-to-all-start.1 = ((bf16[64,2,512]{2,1,0:T(2,128)(2,1)}), bf16[64,2,512]{2,1,0:T(2,128)(2,1)S(1)}, u32[]{:S(2)}, u32[]{:S(2)}) async-start(bf16[64,2,512]{2,1,0:T(2,128)(2,1)} %reshape.202), calls=%async_computation.1 | async-start | bytes 262144 | tf_op jit(solution)/shard_map/all_to_all | solution.py:28
  33.8 5.6 %all-to-all-done.1 = bf16[64,2,512]{2,1,0:T(2,128)(2,1)S(1)} async-done(((bf16[64,2,512]{2,1,0:T(2,128)(2,1)}), bf16[64,2,512]{2,1,0:T(2,128)(2,1)S(1)}, u32[]{:S(2)}, u32[]{:S(2)}) %all-to-all-start.1) | async-done | bytes 131104 | tf_op jit(solution)/shard_map/all_to_all | solution.py:28
  39.8 1.8 gather_fusion.1
  41.7 2.1 convolution_bitcast_fusion.1
  43.7 2.7 %fusion.3 = f32[32,64,128]{2,0,1:T(8,128)S(1)} fusion(f32[64,72,128]{2,0,1:T(8,128)S(1)} %convolution_bitcast_fusion.1, f32[72]{0:T(128)S(1)} %compare_convert_fusion, s32[72]{0:T(128)S(1)} %get-tuple-element.29), kind=kOutput, calls=%fused_computation.11 | convolution fusion | flops 226497024 | bytes 3408448 | tf_op jit(solution)/shard_map/ftd,tb->fbd/dot_general | solution.py:60
  49.1 4.7 %all-to-all-start.2 = ((bf16[64,2,512]{2,1,0:T(2,128)(2,1)}), bf16[64,2,512]{2,1,0:T(2,128)(2,1)S(1)}, u32[]{:S(2)}, u32[]{:S(2)}) async-start(bf16[64,2,512]{2,1,0:T(2,128)(2,1)} %reshape.204), calls=%async_computation.2 | async-start | bytes 262144 | tf_op jit(solution)/shard_map/all_to_all | solution.py:31
  55.1 9.9 %all-to-all-done.2 = bf16[64,2,512]{2,1,0:T(2,128)(2,1)S(1)} async-done(((bf16[64,2,512]{2,1,0:T(2,128)(2,1)}), bf16[64,2,512]{2,1,0:T(2,128)(2,1)S(1)}, u32[]{:S(2)}, u32[]{:S(2)}) %all-to-all-start.2) | async-done | bytes 131104 | tf_op jit(solution)/shard_map/all_to_all | solution.py:31
  65.0 10.0 %all-to-all-start = ((bf16[8,64,384]{2,1,0:T(8,128)(2,1)}), bf16[8,64,384]{2,1,0:T(8,128)(2,1)}, u32[]{:S(2)}, u32[]{:S(2)}) async-start(bf16[8,64,384]{2,1,0:T(8,128)(2,1)} %bitcast_dynamic-update-slice_fusion), calls=%async_computation | async-start | bytes 786432 | tf_op jit(solution)/shard_map/all_to_all | solution.py:66
  79.7 8.2 %scatter_custom_fusion = f32[64,3072]{0,1:T(8,128)} fusion(f32[64,3072]{0,1:T(8,128)} %copy.83, s32[1024]{0:T(1024)} %bitcast.147, bf16[64,1024]{0,1:T(8,128)(2,1)S(1)} %bitcast.140), kind=kCustom, calls=%fused_computation.42 | custom fusion | flops 131072 | bytes 917504 | tf_op jit(solution)/shard_map/scatter-add | solution.py:39
  90.3 6.6 %all-to-all-start.3 = ((bf16[64,8,384]{2,0,1:T(8,128)(2,1)}), bf16[64,8,384]{2,0,1:T(8,128)(2,1)}, u32[]{:S(2)}, u32[]{:S(2)}) async-start(bf16[64,8,384]{2,0,1:T(8,128)(2,1)} %copy.84), calls=%async_computation.3 | async-start | bytes 786432 | tf_op jit(solution)/shard_map/all_to_all | solution.py:71
  97.2 1.9 copy.85
  99.1 2.4 fusion.19
  101.6 8.9 %all-to-all-done.3 = bf16[64,8,384]{2,0,1:T(8,128)(2,1)} async-done(((bf16[64,8,384]{2,0,1:T(8,128)(2,1)}), bf16[64,8,384]{2,0,1:T(8,128)(2,1)}, u32[]{:S(2)}, u32[]{:S(2)}) %all-to-all-start.3) | async-done | bytes 393248 | tf_op jit(solution)/shard_map/all_to_all | solution.py:71
  110.5 3.1 %multiply_convert_fusion = (bf16[512,384]{0,1:T(8,128)(2,1)}, bf16[512,384]{0,1:T(8,128)(2,1)}) fusion(bf16[512,384]{0,1:T(8,128)(2,1)} %copy.85, f32[384,512]{1,0:T(8,128)} %fusion.19, bf16[512,384]{1,0:T(8,128)(2,1)} %bitcast.26, bf16[2,512,512]{2,1,0:T(8,128)(2,1)} %param.12), kind=kOutput, calls=%fused_computation.30 | convolution fusion | flops 203882496 | bytes 2883584 | tf_op jit(solution)/shard_map/io,iv->ov/dot_general | solution.py:74
  113.6 39.7 %all-gather.3.cloned.1.call-done = bf16[512,3072]{0,1:T(8,128)(2,1)} async-done(((bf16[512,384]{0,1:T(8,128)(2,1)}), bf16[512,3072]{0,1:T(8,128)(2,1)}) %all-gather.3.cloned.1.call-update) | async-done | bytes 3145744 | tf_op jit(solution)/shard_map/all_gather | solution.py:82
  153.3 2.7 %fusion.13 = bf16[1,1,64,512]{3,2,1,0:T(8,128)(2,1)S(1)} fusion(bf16[64,3072]{0,1:T(8,128)(2,1)S(1)} %convert_element_type.61, bf16[512,3072]{0,1:T(8,128)(2,1)} %all-gather.3.cloned.1.call-done), kind=kOutput, calls=%fused_computation.26 | convolution fusion | flops 201359360 | bytes 3604480 | tf_op jit(solution)/shard_map/iv,ov->io/dot_general | solution.py:87
  157.5 3.1 %convolution_convert_fusion = bf16[2,64,3072]{2,1,0:T(8,128)(2,1)S(1)} fusion(bf16[512,3072]{0,1:T(8,128)(2,1)} %all-gather.3.cloned.1.call-done, bf16[2,512,512]{2,1,0:T(8,128)(2,1)} %param.12, s32[]{:T(128)S(6)} %select_n.66), kind=kOutput, calls=%fused_computation.7 | convolution fusion | flops 403046400 | bytes 4063236 | tf_op jit(solution)/shard_map/kio,ov->kiv/dot_general | solution.py:91
  162.0 4.3 %gather_fusion.2 = bf16[1024,64]{1,0:T(8,128)(2,1)} fusion(bf16[64,3072]{0,1:T(8,128)(2,1)S(1)} %copy.87, s32[1024]{0:T(1024)S(1)} %fusion.34), kind=kCustom, calls=%fused_computation.2.clone | custom fusion | bytes 266240 | tf_op jit(solution)/shard_map/jit(_take)/gather | solution.py:25
  168.4 10.4 %all-to-all-start.4 = ((bf16[64,2,512]{2,1,0:T(2,128)(2,1)}), bf16[64,2,512]{2,1,0:T(2,128)(2,1)S(1)}, u32[]{:S(2)}, u32[]{:S(2)}) async-start(bf16[64,2,512]{2,1,0:T(2,128)(2,1)} %reshape.206), calls=%async_computation.4 | async-start | bytes 262144 | tf_op jit(solution)/shard_map/all_to_all | solution.py:28
  178.8 1.9 copy.93
  180.7 9.9 %all-to-all-done.4 = bf16[64,2,512]{2,1,0:T(2,128)(2,1)S(1)} async-done(((bf16[64,2,512]{2,1,0:T(2,128)(2,1)}), bf16[64,2,512]{2,1,0:T(2,128)(2,1)S(1)}, u32[]{:S(2)}, u32[]{:S(2)}) %all-to-all-start.4) | async-done | bytes 131104 | tf_op jit(solution)/shard_map/all_to_all | solution.py:28
  191.1 1.9 gather_fusion.3
  193.0 3.0 %convolution_bitcast_fusion = f32[64,72,128]{2,0,1:T(8,128)S(1)} fusion(bf16[72,128,128]{2,1,0:T(8,128)(2,1)S(1)} %copy-done, bf16[72,64,128]{2,1,0:T(8,128)(2,1)} %gather_fusion.3, pred[72]{0:T(512)(128)(4,1)S(1)} %copy-done.12), kind=kOutput, calls=%fused_computation.13 | convolution fusion | flops 151584768 | bytes 5898312 | tf_op jit(solution)/shard_map/ftd,tsd->fts/dot_general | solution.py:53
  196.0 2.7 %fusion.1 = f32[32,64,128]{2,0,1:T(8,128)S(1)} fusion(f32[64,72,128]{2,0,1:T(8,128)S(1)} %convolution_bitcast_fusion, s32[72]{0:T(128)S(1)} %copy-done.11, f32[72]{0:T(128)S(1)} %copy-done.10), kind=kOutput, calls=%fused_computation.9 | convolution fusion | flops 226497024 | bytes 3408448 | tf_op jit(solution)/shard_map/ftd,tb->fbd/dot_general | solution.py:60
  201.9 4.5 %all-to-all-start.5 = ((bf16[64,2,512]{2,1,0:T(2,128)(2,1)}), bf16[64,2,512]{2,1,0:T(2,128)(2,1)S(1)}, u32[]{:S(2)}, u32[]{:S(2)}) async-start(bf16[64,2,512]{2,1,0:T(2,128)(2,1)} %reshape.208), calls=%async_computation.5 | async-start | bytes 262144 | tf_op jit(solution)/shard_map/all_to_all | solution.py:31
  206.4 2.0 slice_add_fusion
  208.3 2.8 %copy.92 = f32[64,3072]{0,1:T(8,128)} copy(f32[64,3072]{1,0:T(8,128)} %slice_add_fusion) | data formatting | bytes 1572864 | tf_op jit(solution)/shard_map/add
  211.2 6.6 %all-to-all-done.5 = bf16[64,2,512]{2,1,0:T(2,128)(2,1)S(1)} async-done(((bf16[64,2,512]{2,1,0:T(2,128)(2,1)}), bf16[64,2,512]{2,1,0:T(2,128)(2,1)S(1)}, u32[]{:S(2)}, u32[]{:S(2)}) %all-to-all-start.5) | async-done | bytes 131104 | tf_op jit(solution)/shard_map/all_to_all | solution.py:31
  218.0 8.2 %scatter_custom_fusion.1 = f32[64,3072]{0,1:T(8,128)} fusion(f32[64,3072]{0,1:T(8,128)} %copy.92, s32[1024]{0:T(1024)} %bitcast.148, bf16[64,1024]{0,1:T(8,128)(2,1)S(1)} %bitcast.139), kind=kCustom, calls=%fused_computation.40 | custom fusion | flops 131072 | bytes 917504 | tf_op jit(solution)/shard_map/scatter-add | solution.py:39
  228.7 15.6 %all-gather.5.cloned.1.call-done = bf16[64,2,64,512]{3,2,1,0:T(8,128)(2,1)} async-done(((bf16[1,2,64,512]{3,2,1,0:T(8,128)(2,1)}), bf16[64,2,64,512]{3,2,1,0:T(8,128)(2,1)}) %all-gather.5.cloned.1.call-update) | async-done | bytes 8388624 | tf_op jit(solution)/shard_map/all_gather | solution.py:8
  244.3 5.5 %convert_reduce_fusion = f32[2,64,512]{2,1,0:T(8,128)} fusion(bf16[64,2,64,512]{3,2,1,0:T(8,128)(2,1)} %all-gather.5.cloned.1.call-done), kind=kLoop, calls=%fused_computation.6 | loop fusion | flops 8323072 | bytes 8650752 | tf_op jit(solution)/shard_map/reduce_sum | solution.py:9
  (80 shorter events, 33.1 us)
Async XLA Ops:
  7.2 34.5 %copy-start = (bf16[72,128,128]{2,1,0:T(8,128)(2,1)S(1)}, bf16[72,128,128]{2,1,0:T(8,128)(2,1)}, u32[]{:S(2)}) copy-start(bf16[72,128,128]{2,1,0:T(8,128)(2,1)} %param.13) | copy-start | bytes 7077892
  7.2 21.0 %copy-start.2 = (bf16[64,3072]{1,0:T(8,128)(2,1)S(1)}, bf16[64,3072]{1,0:T(8,128)(2,1)}, u32[]{:S(2)}) copy-start(bf16[64,3072]{1,0:T(8,128)(2,1)} %param.11) | copy-start | bytes 1179652
  7.2 21.7 %copy-start.8 = (s32[72,2]{0,1:T(2,128)S(1)}, s32[72,2]{0,1:T(2,128)}, u32[]{:S(2)}) copy-start(s32[72,2]{0,1:T(2,128)} %param.14) | copy-start | bytes 1732
  8.1 0.6 copy-start.6
  16.6 22.7 %all-to-all-start.1 = ((bf16[64,2,512]{2,1,0:T(2,128)(2,1)}), bf16[64,2,512]{2,1,0:T(2,128)(2,1)S(1)}, u32[]{:S(2)}, u32[]{:S(2)}) async-start(bf16[64,2,512]{2,1,0:T(2,128)(2,1)} %reshape.202), calls=%async_computation.1 | async-start | bytes 262144 | tf_op jit(solution)/shard_map/all_to_all | solution.py:28
  33.1 10.6 %copy-start.9 = (f32[72]{0:T(128)}, f32[72]{0:T(128)S(1)}, u32[]{:S(2)}) copy-start(f32[72]{0:T(128)S(1)} %compare_convert_fusion) | copy-start | bytes 868
  46.4 28.6 %copy-start.7 = (s32[1,64,16]{2,1,0:T(8,128)S(1)}, s32[1,64,16]{2,1,0:T(8,128)}, u32[]{:S(2)}) copy-start(s32[1,64,16]{2,1,0:T(8,128)} %copy-done.6) | copy-start | bytes 12292
  47.0 1.0 copy-start.3
  49.1 15.9 %all-to-all-start.2 = ((bf16[64,2,512]{2,1,0:T(2,128)(2,1)}), bf16[64,2,512]{2,1,0:T(2,128)(2,1)S(1)}, u32[]{:S(2)}, u32[]{:S(2)}) async-start(bf16[64,2,512]{2,1,0:T(2,128)(2,1)} %reshape.204), calls=%async_computation.2 | async-start | bytes 262144 | tf_op jit(solution)/shard_map/all_to_all | solution.py:31
  65.0 10.1 %copy-start.5 = (bf16[64,2,512]{2,1,0:T(2,128)(2,1)}, bf16[64,2,512]{2,1,0:T(2,128)(2,1)S(1)}, u32[]{:S(2)}) copy-start(bf16[64,2,512]{2,1,0:T(2,128)(2,1)S(1)} %all-to-all-done.2) | copy-start | bytes 393220
  65.0 25.4 %all-to-all-start = ((bf16[8,64,384]{2,1,0:T(8,128)(2,1)}), bf16[8,64,384]{2,1,0:T(8,128)(2,1)}, u32[]{:S(2)}, u32[]{:S(2)}) async-start(bf16[8,64,384]{2,1,0:T(8,128)(2,1)} %bitcast_dynamic-update-slice_fusion), calls=%async_computation | async-start | bytes 786432 | tf_op jit(solution)/shard_map/all_to_all | solution.py:66
  90.3 20.1 %all-to-all-start.3 = ((bf16[64,8,384]{2,0,1:T(8,128)(2,1)}), bf16[64,8,384]{2,0,1:T(8,128)(2,1)}, u32[]{:S(2)}, u32[]{:S(2)}) async-start(bf16[64,8,384]{2,0,1:T(8,128)(2,1)} %copy.84), calls=%async_computation.3 | async-start | bytes 786432 | tf_op jit(solution)/shard_map/all_to_all | solution.py:71
  97.0 56.4 %all-gather.3.cloned.1.call-start = ((), (), s32[]{:S(2)}) async-start(), calls=%async_computation.6 | async-start | bytes 3538944 | tf_op jit(solution)/shard_map/all_gather | solution.py:82
  113.6 130.7 %all-gather.5.cloned.1.call-start = ((), (), s32[]{:S(2)}) async-start(), calls=%async_computation.7 | async-start | bytes 8519680 | tf_op jit(solution)/shard_map/all_gather | solution.py:8
  153.3 2.8 %copy-start.1 = (bf16[512,3072]{0,1:T(8,128)(2,1)S(1)}, bf16[512,3072]{0,1:T(8,128)(2,1)}, u32[]{:S(2)}) copy-start(bf16[512,3072]{0,1:T(8,128)(2,1)} %all-gather.3.cloned.1.call-done) | copy-start | bytes 9437188
  160.7 0.9 copy-start.4
  168.4 22.2 %all-to-all-start.4 = ((bf16[64,2,512]{2,1,0:T(2,128)(2,1)}), bf16[64,2,512]{2,1,0:T(2,128)(2,1)S(1)}, u32[]{:S(2)}, u32[]{:S(2)}) async-start(bf16[64,2,512]{2,1,0:T(2,128)(2,1)} %reshape.206), calls=%async_computation.4 | async-start | bytes 262144 | tf_op jit(solution)/shard_map/all_to_all | solution.py:28
  178.8 14.2 %copy-start.12 = (pred[72]{0:T(512)(128)(4,1)S(1)}, pred[72]{0:T(512)(128)(4,1)}, u32[]{:S(2)}) copy-start(pred[72]{0:T(512)(128)(4,1)} %get-tuple-element.20) | copy-start | bytes 220
  193.0 3.0 %copy-start.10 = (f32[72]{0:T(128)S(1)}, f32[72]{0:T(128)}, u32[]{:S(2)}) copy-start(f32[72]{0:T(128)} %copy-done.9) | copy-start | bytes 868
  193.0 3.0 %copy-start.11 = (s32[72]{0:T(128)S(1)}, s32[72]{0:T(128)}, u32[]{:S(2)}) copy-start(s32[72]{0:T(128)} %get-tuple-element.28) | copy-start | bytes 868
  201.9 15.8 %all-to-all-start.5 = ((bf16[64,2,512]{2,1,0:T(2,128)(2,1)}), bf16[64,2,512]{2,1,0:T(2,128)(2,1)S(1)}, u32[]{:S(2)}, u32[]{:S(2)}) async-start(bf16[64,2,512]{2,1,0:T(2,128)(2,1)} %reshape.208), calls=%async_computation.5 | async-start | bytes 262144 | tf_op jit(solution)/shard_map/all_to_all | solution.py:31
Sparse Core Ops, SparseCore 0:
  113.7 39.6 all-gather.2
  157.6 86.6 all-gather.4
